TPU v7x, 512 devices: a whole 4x8x8 slice. The times are simulated.
512 devices in a mesh: exp: 64 (over x, y, core), rep: 8 (over z).
Axes of the slice: x: 4, y: 8, z: 8, core: 2. Of those that a mesh axis runs over, the one named last changes fastest.
Arguments:
- passages_in: bfloat16 [92160, 2048], P(('exp', 'rep')), may hold values from -24 to 32
- routes: int32 [92160, 2], P(('exp', 'rep')), may hold values from 0 to 63, all different within a row; in each aligned block of 180 rows (0 to 179, 180 to 359, ...) at most 11 rows name the same one
- route_weights: float32 [92160, 2], P(('exp', 'rep')), may hold values from 0.2 to 1
- gate_weight: bfloat16 [64, 2048, 704], P('exp', 'rep'), may hold values from -0.125 to 0.125
- up_weight: bfloat16 [64, 2048, 704], P('exp', 'rep'), may hold values from -0.125 to 0.125
- down_weight: bfloat16 [64, 704, 2048], P('exp', None, 'rep'), may hold values from -0.21875 to 0.21875
- projection: bfloat16 [2048, 128], replicated, may hold values from -2 to 2
- queries: bfloat16 [128, 32, 128], P('rep'), may hold values from -6 to 6
- positives: int32 [128], replicated, may hold values from 0 to 511, as said below
Outputs:
- states: bfloat16 [92160, 2048], P(('exp', 'rep'))
- grad_projection: float32 [2048, 128], P('exp')
- mean_loss: float32 [], replicated
Inputs may be any that keep to these rules, and one draw needn't show every extreme that they name: `routes`: the two experts of a token differ. Among the rows of one device, no expert is named more than 11 times, and in some device's rows some expert is named exactly 11 times; every expert is named somewhere. `positives`: distinct queries have distinct positive passages.
All inputs are finite; a program needn't handle non-finite values.
Results may differ from a plain program's by a relative error of at most 0.0065.
Values may be sent and summed in bfloat16 or wider, within the bound.
No kernel may reach another device: no remote copies, remote signals or barrier semaphores. Data moves between devices by JAX's collectives and lax.ppermute only.
A program may use at most 64 MiB of HBM per device.

v0:
```python
import jax
import jax.numpy as jnp
from jax import lax
from jax.sharding import PartitionSpec as P

PAS_LEN = 180
soft_temp = 0.05
logit_gain = 1.5
norm_eps = 1e-06


def unit_rows(values):
    values = values.astype(jnp.float32)
    radius = jnp.sqrt(jnp.sum(values * values, axis=-1, keepdims=True) + norm_eps)
    return (values / radius, radius)


def token_scores(unit_block, query_rows, passage_count, query_count):
    scores = lax.dot_general(
        unit_block, query_rows, (((1,), (1,)), ((), ())), preferred_element_type=jnp.float32
    )
    weights = jnp.exp(scores / soft_temp)
    passage_len = unit_block.shape[0] // passage_count
    totals = jnp.sum(weights.reshape(passage_count, passage_len, -1), axis=1)
    logits = logit_gain * jnp.sum(
        (soft_temp * jnp.log(totals)).reshape(passage_count, query_count, -1), axis=2
    )
    return (weights, totals, logits)


def unit_grads(weights, totals, factor, query_rows, passage_count, query_count):
    passage_len = weights.shape[0] // passage_count
    query_len = weights.shape[1] // query_count
    shaped = weights.reshape(passage_count, passage_len, query_count, query_len) / totals.reshape(
        passage_count, 1, query_count, query_len
    )
    coeffs = (shaped * (logit_gain * factor)[:, None, :, None]).astype(jnp.bfloat16)
    coeffs = coeffs.reshape(passage_count * passage_len, query_count * query_len)
    return jnp.dot(coeffs, query_rows, preferred_element_type=jnp.float32)


def body(
    passages_in,
    routes,
    route_weights,
    gate_weight,
    up_weight,
    down_weight,
    projection,
    queries,
    positives,
):
    tok_count, model_width = passages_in.shape
    top_count = routes.shape[1]
    experts = lax.axis_size("exp")
    rep_count = lax.axis_size("rep")
    capacity = max(2, 2 * tok_count * top_count // experts)
    flat_route = routes.reshape(-1)
    onehot = (flat_route[:, None] == jnp.arange(experts, dtype=jnp.int32)[None, :]).astype(
        jnp.int32
    )
    slot_rank = jnp.sum((jnp.cumsum(onehot, axis=0) - onehot) * onehot, axis=1)
    places = flat_route * capacity + slot_rank
    sources = jnp.arange(tok_count * top_count, dtype=jnp.int32) // top_count
    outgoing = (
        jnp.zeros((experts * capacity, model_width), jnp.bfloat16)
        .at[places]
        .set(passages_in[sources])
    )
    arrived = lax.all_to_all(
        outgoing.reshape(experts, capacity, model_width),
        "exp",
        split_axis=0,
        concat_axis=0,
        tiled=True,
    )
    expert_rows = arrived.reshape(experts * capacity, model_width)

    def add_rows(shard_part):
        return jnp.dot(expert_rows, shard_part[0], preferred_element_type=jnp.float32)

    gate_sum = add_rows(lax.all_gather(gate_weight, "rep", axis=1, tiled=True))
    up_sum = add_rows(lax.all_gather(up_weight, "rep", axis=1, tiled=True))
    hidden = (jax.nn.silu(gate_sum) * up_sum).astype(jnp.bfloat16)
    expert_out = jnp.dot(
        hidden,
        lax.all_gather(down_weight, "rep", axis=2, tiled=True)[0],
        preferred_element_type=jnp.float32,
    ).astype(jnp.bfloat16)
    returned = lax.all_to_all(
        expert_out.reshape(experts, capacity, model_width),
        "exp",
        split_axis=0,
        concat_axis=0,
        tiled=True,
    )
    picked = returned.reshape(experts * capacity, model_width)[places].reshape(
        tok_count, top_count, model_width
    )
    mixed_sum = passages_in.astype(jnp.float32) + jnp.sum(
        route_weights[:, :, None] * picked.astype(jnp.float32), axis=1
    )
    states = mixed_sum.astype(jnp.bfloat16)
    projected = jnp.dot(states, projection, preferred_element_type=jnp.float32)
    unit_f32, radius = unit_rows(projected)
    unit_vec = unit_f32.astype(jnp.bfloat16)
    query_unit = unit_rows(queries)[0].astype(jnp.bfloat16)
    query_block, query_len, unit_width = queries.shape
    pas_count = tok_count // PAS_LEN
    total_queries = query_block * rep_count
    all_queries = lax.all_gather(query_unit, "rep", axis=0, tiled=True)
    query_rows = all_queries.reshape(total_queries * query_len, unit_width)
    owners = lax.axis_index(("exp", "rep")) * pas_count + jnp.arange(pas_count, dtype=jnp.int32)
    weights, totals, logits = token_scores(unit_vec, query_rows, pas_count, total_queries)
    positive_hit = owners[:, None] == positives[None, :]
    exp_logits = jnp.exp(logits)
    partition, pos_sum = lax.psum(
        (jnp.sum(exp_logits, axis=0), jnp.sum(jnp.where(positive_hit, logits, 0.0))), ("exp", "rep")
    )
    mean_loss = (jnp.sum(jnp.log(partition)) - pos_sum) / total_queries
    factor = exp_logits / partition[None, :] - positive_hit.astype(jnp.float32)
    grad_unit = unit_grads(weights, totals, factor, query_rows, pas_count, total_queries)
    grad_vec = (
        (grad_unit - unit_f32 * jnp.sum(unit_f32 * grad_unit, axis=1, keepdims=True)) / radius
    ).astype(jnp.bfloat16)
    row_sums = lax.psum_scatter(
        lax.dot_general(
            states, grad_vec, (((0,), (0,)), ((), ())), preferred_element_type=jnp.float32
        ),
        "exp",
        scatter_dimension=0,
        tiled=True,
    )
    grad_projection = lax.psum(row_sums, "rep")
    return (states, grad_projection, mean_loss)


def solution(mesh):
    in_specs = (
        P(("exp", "rep"), None),
        P(("exp", "rep"), None),
        P(("exp", "rep"), None),
        P("exp", "rep", None),
        P("exp", "rep", None),
        P("exp", None, "rep"),
        P(),
        P("rep", None, None),
        P(),
    )
    out_specs = (P(("exp", "rep"), None), P("exp", None), P())
    return jax.shard_map(body, mesh=mesh, in_specs=in_specs, out_specs=out_specs, check_vma=False)
```

profile of v0, /device:TPU:16, one launch (start us, length us, event | category | flops | bytes accessed | tf_op | source)
XLA Modules:
  0.0 605.3 jit_solution(8828364484753994428)
XLA Ops:
  8.7 0.8 copy.20
  9.7 0.9 reduce-window.6
  12.0 8.1 %scatter_custom_fusion = bf16[704,2048]{1,0:T(8,128)(2,1)S(1)} fusion(s32[360]{0:T(512)S(1)} %fusion.22, bf16[180,2048]{1,0:T(8,128)(2,1)} %param.9, s32[1024]{0:T(1024)S(1)} %pad_clamp_fusion.1, bf16[]{:T(256)} %constant.21.clone.1), kind=kCustom, calls=%fused_computation.16 | custom fusion | bytes 2884096 | tf_op jit(solution)/shard_map/scatter | solution.py:68
  20.1 2.9 reshape.185
  23.0 10.8 %all-to-all-start = ((bf16[64,11,2048]{2,1,0:T(8,128)(2,1)}), bf16[64,11,2048]{2,1,0:T(8,128)(2,1)}, u32[]{:S(2)}, u32[]{:S(2)}) async-start(bf16[64,11,2048]{2,1,0:T(8,128)(2,1)} %reshape.185), calls=%async_computation | async-start | bytes 8388608 | tf_op jit(solution)/shard_map/all_to_all | solution.py:70
  34.5 93.6 %all-to-all-done = bf16[64,11,2048]{2,1,0:T(8,128)(2,1)} async-done(((bf16[64,11,2048]{2,1,0:T(8,128)(2,1)}), bf16[64,11,2048]{2,1,0:T(8,128)(2,1)}, u32[]{:S(2)}, u32[]{:S(2)}) %all-to-all-start) | async-done | bytes 2883616 | tf_op jit(solution)/shard_map/all_to_all | solution.py:70
  128.1 3.4 reshape.186
  131.5 5.6 fusion.4
  137.1 44.8 %all-gather.9.cloned.1.call-done = bf16[1,704,2048]{2,1,0:T(8,128)(2,1)} async-done(((bf16[1,704,256]{2,1,0:T(8,128)(2,1)}), bf16[1,704,2048]{2,1,0:T(8,128)(2,1)}) %all-gather.9.cloned.1.call-update) | async-done | bytes 2883600 | tf_op jit(solution)/shard_map/all_gather | solution.py:87
  181.9 10.4 %convolution_convert_fusion = bf16[704,2048]{1,0:T(8,128)(2,1)} fusion(bf16[1,704,2048]{2,1,0:T(8,128)(2,1)} %all-gather.9.cloned.1.call-done, f32[704,704]{1,0:T(8,128)} %fusion.4, bf16[704,2048]{1,0:T(8,128)(2,1)S(1)} %reshape.186, bf16[1,2048,704]{1,2,0:T(8,128)(2,1)} %all-gather.7.cloned.1.call-done), kind=kOutput, calls=%fused_computation.5 | convolution fusion | flops 4064501760 | bytes 13516800 | tf_op jit(solution)/shard_map/dot_general | solution.py:85
  192.3 4.8 reshape.187
  197.1 10.5 %all-to-all-start.1 = ((bf16[64,11,2048]{2,1,0:T(8,128)(2,1)}), bf16[64,11,2048]{2,1,0:T(8,128)(2,1)}, u32[]{:S(2)}, u32[]{:S(2)}) async-start(bf16[64,11,2048]{2,1,0:T(8,128)(2,1)} %reshape.187), calls=%async_computation.1 | async-start | bytes 8388608 | tf_op jit(solution)/shard_map/all_to_all | solution.py:90
  207.8 0.8 fusion.15
  209.7 92.1 %all-to-all-done.1 = bf16[64,11,2048]{2,1,0:T(8,128)(2,1)} async-done(((bf16[64,11,2048]{2,1,0:T(8,128)(2,1)}), bf16[64,11,2048]{2,1,0:T(8,128)(2,1)}, u32[]{:S(2)}, u32[]{:S(2)}) %all-to-all-start.1) | async-done | bytes 2883616 | tf_op jit(solution)/shard_map/all_to_all | solution.py:90
  301.9 3.4 reshape.188
  305.3 3.1 gather_fusion
  308.4 3.4 reshape.191
  311.8 5.6 multiply_reduce_fusion
  318.0 3.8 fusion.28
  322.7 96.3 %all-reduce.1 = (f32[128]{0:T(128)S(1)}, f32[]{:T(128)}) all-reduce(f32[128]{0:T(128)S(1)} %get-tuple-element.8, f32[]{:T(128)} %get-tuple-element.7), channel_id=1, replica_groups=mesh['exp'=64,'rep'=8] {'exp','rep'}, use_global_device_ids=true, to_apply=%region_9.10 | all-reduce | flops 129 | bytes 1032 | tf_op jit(solution)/shard_map/psum | solution.py:117
  419.7 2.5 multiply_reduce_fusion.1
  422.2 1.6 fusion.18
  425.1 141.1 %reduce-scatter.2.cloned.1.call-done = f32[32,128]{1,0:T(8,128)} async-done(((f32[2048,128]{1,0:T(8,128)}), f32[32,128]{1,0:T(8,128)}) %reduce-scatter.2.cloned.1.call-update) | async-done | bytes 16400 | tf_op jit(solution)/shard_map/reduce_scatter | solution.py:126
  566.2 31.5 %psum.22 = f32[32,128]{1,0:T(8,128)} all-reduce(f32[32,128]{1,0:T(8,128)} %reduce-scatter.2.cloned.1.call-done), channel_id=1, replica_groups=mesh['exp'=64,'rep'=8] {'rep'}, use_global_device_ids=true, to_apply=%region_12.13 | all-reduce | flops 4096 | bytes 32768 | tf_op jit(solution)/shard_map/psum | solution.py:134
  (54 shorter events, 7.3 us)
Async XLA Ops:
  7.2 310.3 %copy-start = (bf16[2048,128]{1,0:T(8,128)(2,1)S(1)}, bf16[2048,128]{1,0:T(8,128)(2,1)}, u32[]{:S(2)}) copy-start(bf16[2048,128]{1,0:T(8,128)(2,1)} %param.15) | copy-start | bytes 1572868
  7.2 124.3 %all-gather.5.cloned.1.call-start = ((), (), s32[]{:S(2)}) async-start(), calls=%async_computation.3 | async-start | bytes 3244032 | tf_op jit(solution)/shard_map/all_gather | solution.py:82
  7.9 129.2 %all-gather.7.cloned.1.call-start = ((), (), s32[]{:S(2)}) async-start(), calls=%async_computation.4 | async-start | bytes 3244032 | tf_op jit(solution)/shard_map/all_gather | solution.py:83
  23.0 105.1 %all-to-all-start = ((bf16[64,11,2048]{2,1,0:T(8,128)(2,1)}), bf16[64,11,2048]{2,1,0:T(8,128)(2,1)}, u32[]{:S(2)}, u32[]{:S(2)}) async-start(bf16[64,11,2048]{2,1,0:T(8,128)(2,1)} %reshape.185), calls=%async_computation | async-start | bytes 8388608 | tf_op jit(solution)/shard_map/all_to_all | solution.py:70
  33.7 148.2 %all-gather.9.cloned.1.call-start = ((), (), s32[]{:S(2)}) async-start(), calls=%async_computation.5 | async-start | bytes 3244032 | tf_op jit(solution)/shard_map/all_gather | solution.py:87
  197.1 10.6 %copy-start.4 = (bf16[16,32,128]{2,1,0:T(8,128)(2,1)S(1)}, bf16[16,32,128]{2,1,0:T(8,128)(2,1)}, u32[]{:S(2)}) copy-start(bf16[16,32,128]{2,1,0:T(8,128)(2,1)} %param.16) | copy-start | bytes 393220
  197.1 11.9 %copy-start.5 = (f32[180,2]{0,1:T(2,128)S(1)}, f32[180,2]{0,1:T(2,128)}, u32[]{:S(2)}) copy-start(f32[180,2]{0,1:T(2,128)} %param.11) | copy-start | bytes 4324
  197.1 104.8 %all-to-all-start.1 = ((bf16[64,11,2048]{2,1,0:T(8,128)(2,1)}), bf16[64,11,2048]{2,1,0:T(8,128)(2,1)}, u32[]{:S(2)}, u32[]{:S(2)}) async-start(bf16[64,11,2048]{2,1,0:T(8,128)(2,1)} %reshape.187), calls=%async_computation.1 | async-start | bytes 8388608 | tf_op jit(solution)/shard_map/all_to_all | solution.py:90
  207.6 110.4 %all-gather.11.cloned.1.call-start = ((), (), s32[]{:S(2)}) async-start(), calls=%async_computation.6 | async-start | bytes 1179648 | tf_op jit(solution)/shard_map/all_gather | solution.py:111
  208.7 357.5 %reduce-scatter.2.cloned.1.call-start = ((), (), s32[]{:S(2)}) async-start(), calls=%async_computation.7 | async-start | bytes 1064960 | tf_op jit(solution)/shard_map/reduce_scatter | solution.py:126
  311.7 5.6 copy-start.3
  317.5 104.7 %copy-start.1 = (bf16[180,2048]{1,0:T(8,128)(2,1)}, bf16[180,2048]{1,0:T(8,128)(2,1)S(1)}, u32[]{:S(2)}) copy-start(bf16[180,2048]{1,0:T(8,128)(2,1)S(1)} %add_convert_fusion) | copy-start | bytes 2211844
  317.5 4.5 copy-start.6
  318.0 101.6 %copy-start.2 = (bf16[128,32,128]{2,1,0:T(8,128)(2,1)S(1)}, bf16[128,32,128]{2,1,0:T(8,128)(2,1)}, u32[]{:S(2)}) copy-start(bf16[128,32,128]{2,1,0:T(8,128)(2,1)} %all-gather.11.cloned.1.call-done) | copy-start | bytes 3145732
Sparse Core Ops, SparseCore 0:
  10.0 59.7 all-gather.4
  71.8 53.6 all-gather.6
  127.5 54.4 all-gather.8
  210.2 40.1 all-gather.10
  423.9 142.2 reduce-scatter.1
where the time goes:
time: 606 us; the launch traced here: 605 us
  waiting for transfers between devices  374 us (62%)
  blocking collectives  128 us (21%)
  local copies, waits for them, and re-layouts  31.4 us (5%)
  matrix products  24.3 us (4%)
  starting transfers between devices  21.9 us (4%)
  between operations  16.5 us (3%)
  other arithmetic  9.89 us (2%)
    reduce_scatter x1, waiting for transfers between devices, body(): lax.psum_scatter(lax.dot_general(states, grad_vec, (((0,), (0,)), ((), ()...  141 us
    psum x1, blocking collectives, body(): lax.psum((jnp.sum(exp_logits, axis=0), jnp.sum(jnp.where(positive_hit, lo...  96.3 us
    all_to_all x1, waiting for transfers between devices, body(): lax.all_to_all(outgoing.reshape(experts, capacity, model_width), 'exp', s...  93.6 us
    all_to_all x1, waiting for transfers between devices, body(): lax.all_to_all(expert_out.reshape(experts, capacity, model_width), 'exp',...  92.1 us
    all_gather x1, waiting for transfers between devices, body(): lax.all_gather(down_weight, 'rep', axis=2, tiled=True)[0]  44.8 us
    psum x1, blocking collectives, body(): grad_projection = lax.psum(row_sums, 'rep')  31.5 us
  transfers between devices with their start and end apart: 7, of which 4 were waited for; matrix products, arithmetic and copies ran while one was open for 7% of the time, Pallas kernels for 0%

commit v1 on v0

--- a/solution.py
+++ b/solution.py
@@ -84,7 +84,9 @@
     hidden = (jax.nn.silu(gate_sum) * up_sum).astype(jnp.bfloat16)
     expert_out = jnp.dot(
         hidden,
-        lax.all_gather(down_weight, "rep", axis=2, tiled=True)[0],
+        jnp.concatenate(
+            lax.all_to_all(jnp.stack([down_weight] * lax.axis_size("rep")), "rep", 0, 0), axis=2
+        )[0],
         preferred_element_type=jnp.float32,
     ).astype(jnp.bfloat16)
     returned = lax.all_to_all(

time: 606 us -> 640 us (1.056)
  waiting for transfers between devices: 374 us -> 394 us
  starting transfers between devices: 21.9 us -> 31.3 us
    all_to_all x0 -> x1, waiting for transfers between devices: none -> 68.1 us  [body(): lax.all_to_all(jnp.stack([down_weight] * lax.axis_size('rep')), 'rep', 0, 0)]
    all_gather x1 -> x0, waiting for transfers between devices: 44.8 us -> none  [body(): lax.all_gather(down_weight, 'rep', axis=2, tiled=True)[0]]
    all_to_all x0 -> x1, starting transfers between devices: none -> 10.4 us  [body(): lax.all_to_all(jnp.stack([down_weight] * lax.axis_size('rep')), 'rep', 0, 0)]
where the time goes in v1:
time: 640 us; the launch traced here: 639 us
  waiting for transfers between devices  394 us (62%)
  blocking collectives  126 us (20%)
  local copies, waits for them, and re-layouts  37.4 us (6%)
  starting transfers between devices  31.3 us (5%)
  matrix products  24.2 us (4%)
  between operations  16.5 us (3%)
  other arithmetic  9.2 us (1%)
    reduce_scatter x1, waiting for transfers between devices, body(): lax.psum_scatter(lax.dot_general(states, grad_vec, (((0,), (0,)), ((), ()...  143 us
    psum x1, blocking collectives, body(): lax.psum((jnp.sum(exp_logits, axis=0), jnp.sum(jnp.where(positive_hit, lo...  95.1 us
    all_to_all x1, waiting for transfers between devices, body(): lax.all_to_all(expert_out.reshape(experts, capacity, model_width), 'exp',...  92.1 us
    all_to_all x1, waiting for transfers between devices, body(): lax.all_to_all(outgoing.reshape(experts, capacity, model_width), 'exp', s...  89.7 us
    all_to_all x1, waiting for transfers between devices, body(): lax.all_to_all(jnp.stack([down_weight] * lax.axis_size('rep')), 'rep', 0, 0)  68.1 us
    psum x1, blocking collectives, body(): grad_projection = lax.psum(row_sums, 'rep')  31.4 us
  transfers between devices with their start and end apart: 7, of which 4 were waited for; matrix products, arithmetic and copies ran while one was open for 7% of the time, Pallas kernels for 0%

profile of v1, /device:TPU:16, one launch (start us, length us, event | category | flops | bytes accessed | tf_op | source)
XLA Modules:
  0.0 639.1 jit_solution(17005552341865607009)
XLA Ops:
  7.2 2.8 stack.2
  10.0 10.4 %all-to-all-start.1 = ((bf16[8,1,704,256]{3,2,1,0:T(8,128)(2,1)}), bf16[8,1,704,256]{3,2,1,0:T(8,128)(2,1)}, u32[]{:S(2)}, u32[]{:S(2)}) async-start(bf16[8,1,704,256]{3,2,1,0:T(8,128)(2,1)} %stack.2), calls=%async_computation.1 | async-start | bytes 5767168 | tf_op jit(solution)/shard_map/all_to_all | solution.py:88
  23.2 8.2 %scatter_custom_fusion = bf16[704,2048]{1,0:T(8,128)(2,1)S(1)} fusion(s32[360]{0:T(512)S(1)} %fusion.21, bf16[180,2048]{1,0:T(8,128)(2,1)} %param.9, s32[1024]{0:T(1024)S(1)} %pad_clamp_fusion.1, bf16[]{:T(256)} %constant.21.clone.1), kind=kCustom, calls=%fused_computation.15 | custom fusion | bytes 2884096 | tf_op jit(solution)/shard_map/scatter | solution.py:68
  31.3 2.9 reshape.191
  34.2 68.1 %all-to-all-done.1 = bf16[8,1,704,256]{3,2,1,0:T(8,128)(2,1)} async-done(((bf16[8,1,704,256]{3,2,1,0:T(8,128)(2,1)}), bf16[8,1,704,256]{3,2,1,0:T(8,128)(2,1)}, u32[]{:S(2)}, u32[]{:S(2)}) %all-to-all-start.1) | async-done | bytes 2883616 | tf_op jit(solution)/shard_map/all_to_all | solution.py:88
  102.3 12.6 %all-to-all-start = ((bf16[64,11,2048]{2,1,0:T(8,128)(2,1)}), bf16[64,11,2048]{2,1,0:T(8,128)(2,1)}, u32[]{:S(2)}, u32[]{:S(2)}) async-start(bf16[64,11,2048]{2,1,0:T(8,128)(2,1)} %reshape.191), calls=%async_computation | async-start | bytes 8388608 | tf_op jit(solution)/shard_map/all_to_all | solution.py:70
  115.6 3.7 copy.26
  119.4 89.7 %all-to-all-done = bf16[64,11,2048]{2,1,0:T(8,128)(2,1)} async-done(((bf16[64,11,2048]{2,1,0:T(8,128)(2,1)}), bf16[64,11,2048]{2,1,0:T(8,128)(2,1)}, u32[]{:S(2)}, u32[]{:S(2)}) %all-to-all-start) | async-done | bytes 2883616 | tf_op jit(solution)/shard_map/all_to_all | solution.py:70
  209.1 3.4 reshape.192
  212.6 5.6 fusion.3
  218.2 10.3 %convolution_convert_fusion = bf16[704,2048]{1,0:T(8,128)(2,1)} fusion(bf16[704,2048]{1,0:T(8,128)(2,1)} %bitcast.39, f32[704,704]{1,0:T(8,128)} %fusion.3, bf16[704,2048]{1,0:T(8,128)(2,1)S(1)} %reshape.192, bf16[1,2048,704]{1,2,0:T(8,128)(2,1)} %all-gather.6.cloned.1.call-done), kind=kOutput, calls=%fused_computation.5 | convolution fusion | flops 4064501760 | bytes 13516800 | tf_op jit(solution)/shard_map/dot_general | solution.py:85
  228.5 4.8 reshape.194
  233.2 7.7 %all-to-all-start.2 = ((bf16[64,11,2048]{2,1,0:T(8,128)(2,1)}), bf16[64,11,2048]{2,1,0:T(8,128)(2,1)}, u32[]{:S(2)}, u32[]{:S(2)}) async-start(bf16[64,11,2048]{2,1,0:T(8,128)(2,1)} %reshape.194), calls=%async_computation.2 | async-start | bytes 8388608 | tf_op jit(solution)/shard_map/all_to_all | solution.py:92
  243.1 92.1 %all-to-all-done.2 = bf16[64,11,2048]{2,1,0:T(8,128)(2,1)} async-done(((bf16[64,11,2048]{2,1,0:T(8,128)(2,1)}), bf16[64,11,2048]{2,1,0:T(8,128)(2,1)}, u32[]{:S(2)}, u32[]{:S(2)}) %all-to-all-start.2) | async-done | bytes 2883616 | tf_op jit(solution)/shard_map/all_to_all | solution.py:92
  335.2 3.4 reshape.195
  338.6 3.1 gather_fusion
  341.7 3.4 reshape.198
  345.1 5.6 multiply_reduce_fusion
  351.4 3.8 fusion.27
  356.0 95.1 %all-reduce.1 = (f32[128]{0:T(128)S(1)}, f32[]{:T(128)}) all-reduce(f32[128]{0:T(128)S(1)} %get-tuple-element.8, f32[]{:T(128)} %get-tuple-element.7), channel_id=1, replica_groups=mesh['exp'=64,'rep'=8] {'exp','rep'}, use_global_device_ids=true, to_apply=%region_9.10 | all-reduce | flops 129 | bytes 1032 | tf_op jit(solution)/shard_map/psum | solution.py:119
  451.9 2.5 multiply_reduce_fusion.1
  454.4 1.6 fusion.17
  457.3 142.8 %reduce-scatter.2.cloned.1.call-done = f32[32,128]{1,0:T(8,128)} async-done(((f32[2048,128]{1,0:T(8,128)}), f32[32,128]{1,0:T(8,128)}) %reduce-scatter.2.cloned.1.call-update) | async-done | bytes 16400 | tf_op jit(solution)/shard_map/reduce_scatter | solution.py:128
  600.1 31.4 %psum.22 = f32[32,128]{1,0:T(8,128)} all-reduce(f32[32,128]{1,0:T(8,128)} %reduce-scatter.2.cloned.1.call-done), channel_id=1, replica_groups=mesh['exp'=64,'rep'=8] {'rep'}, use_global_device_ids=true, to_apply=%region_12.13 | all-reduce | flops 4096 | bytes 32768 | tf_op jit(solution)/shard_map/psum | solution.py:136
  (57 shorter events, 7.7 us)
Async XLA Ops:
  7.2 343.7 %copy-start = (bf16[2048,128]{1,0:T(8,128)(2,1)S(1)}, bf16[2048,128]{1,0:T(8,128)(2,1)}, u32[]{:S(2)}) copy-start(bf16[2048,128]{1,0:T(8,128)(2,1)} %param.15) | copy-start | bytes 1572868
  10.0 11.2 %copy-start.5 = (s32[180,2]{0,1:T(2,128)S(1)}, s32[180,2]{0,1:T(2,128)}, u32[]{:S(2)}) copy-start(s32[180,2]{0,1:T(2,128)} %param.10) | copy-start | bytes 4324
  10.0 92.3 %all-to-all-start.1 = ((bf16[8,1,704,256]{3,2,1,0:T(8,128)(2,1)}), bf16[8,1,704,256]{3,2,1,0:T(8,128)(2,1)}, u32[]{:S(2)}, u32[]{:S(2)}) async-start(bf16[8,1,704,256]{3,2,1,0:T(8,128)(2,1)} %stack.2), calls=%async_computation.1 | async-start | bytes 5767168 | tf_op jit(solution)/shard_map/all_to_all | solution.py:88
  20.5 192.1 %all-gather.4.cloned.1.call-start = ((), (), s32[]{:S(2)}) async-start(), calls=%async_computation.4 | async-start | bytes 3244032 | tf_op jit(solution)/shard_map/all_gather | solution.py:82
  102.3 106.8 %all-to-all-start = ((bf16[64,11,2048]{2,1,0:T(8,128)(2,1)}), bf16[64,11,2048]{2,1,0:T(8,128)(2,1)}, u32[]{:S(2)}, u32[]{:S(2)}) async-start(bf16[64,11,2048]{2,1,0:T(8,128)(2,1)} %reshape.191), calls=%async_computation | async-start | bytes 8388608 | tf_op jit(solution)/shard_map/all_to_all | solution.py:70
  114.9 103.3 %all-gather.6.cloned.1.call-start = ((), (), s32[]{:S(2)}) async-start(), calls=%async_computation.5 | async-start | bytes 3244032 | tf_op jit(solution)/shard_map/all_gather | solution.py:83
  233.2 7.8 %copy-start.4 = (bf16[16,32,128]{2,1,0:T(8,128)(2,1)S(1)}, bf16[16,32,128]{2,1,0:T(8,128)(2,1)}, u32[]{:S(2)}) copy-start(bf16[16,32,128]{2,1,0:T(8,128)(2,1)} %param.16) | copy-start | bytes 393220
  233.2 9.0 %copy-start.6 = (f32[180,2]{0,1:T(2,128)S(1)}, f32[180,2]{0,1:T(2,128)}, u32[]{:S(2)}) copy-start(f32[180,2]{0,1:T(2,128)} %param.11) | copy-start | bytes 4324
  233.2 102.0 %all-to-all-start.2 = ((bf16[64,11,2048]{2,1,0:T(8,128)(2,1)}), bf16[64,11,2048]{2,1,0:T(8,128)(2,1)}, u32[]{:S(2)}, u32[]{:S(2)}) async-start(bf16[64,11,2048]{2,1,0:T(8,128)(2,1)} %reshape.194), calls=%async_computation.2 | async-start | bytes 8388608 | tf_op jit(solution)/shard_map/all_to_all | solution.py:92
  241.0 110.4 %all-gather.8.cloned.1.call-start = ((), (), s32[]{:S(2)}) async-start(), calls=%async_computation.6 | async-start | bytes 1179648 | tf_op jit(solution)/shard_map/all_gather | solution.py:113
  242.0 358.1 %reduce-scatter.2.cloned.1.call-start = ((), (), s32[]{:S(2)}) async-start(), calls=%async_computation.7 | async-start | bytes 1064960 | tf_op jit(solution)/shard_map/reduce_scatter | solution.py:128
  345.1 5.6 copy-start.3
  350.9 103.6 %copy-start.1 = (bf16[180,2048]{1,0:T(8,128)(2,1)}, bf16[180,2048]{1,0:T(8,128)(2,1)S(1)}, u32[]{:S(2)}) copy-start(bf16[180,2048]{1,0:T(8,128)(2,1)S(1)} %add_convert_fusion) | copy-start | bytes 2211844
  350.9 4.5 copy-start.7
  351.4 100.5 %copy-start.2 = (bf16[128,32,128]{2,1,0:T(8,128)(2,1)S(1)}, bf16[128,32,128]{2,1,0:T(8,128)(2,1)}, u32[]{:S(2)}) copy-start(bf16[128,32,128]{2,1,0:T(8,128)(2,1)} %all-gather.8.cloned.1.call-done) | copy-start | bytes 3145732
Sparse Core Ops, SparseCore 0:
  23.3 97.3 all-gather.3
  122.7 51.7 all-gather.5
  243.9 39.0 all-gather.7
  456.1 143.9 reduce-scatter.1
